TPU v7x, 32 devices: a whole 2x2x4 slice. The times are simulated.
32 devices in a mesh: dp: 8 (over y, x, core), ctx: 4 (over z).
Axes of the slice: x: 2, y: 2, z: 4, core: 2. Of those that a mesh axis runs over, the one named last changes fastest.
Arguments:
- queries: bfloat16 [4096, 32, 128], P(('ctx', 'dp')), may hold values from -8 to 8
- keys: bfloat16 [4096, 8, 128], P(('ctx', 'dp')), may hold values from -8 to 8
- values: bfloat16 [4096, 8, 128], P(('ctx', 'dp')), may hold values from -6 to 6
- doc_blocks: int32 [16], replicated, may hold values from 1 to 4, 32 in all
Outputs:
- attended: bfloat16 [4096, 32, 128], P(('ctx', 'dp'))
Inputs may be any that keep to these rules, and one draw needn't show every extreme that they name: `doc_blocks`: lengths in blocks of 128 tokens; they sum to 32 and the longest is exactly 4.
All inputs are finite; a program needn't handle non-finite values.
Results may differ from a plain program's by a relative error of at most 0.0037.
Values may be sent and summed in bfloat16 or wider, within the bound.
No kernel may reach another device: no remote copies, remote signals or barrier semaphores. Data moves between devices by JAX's collectives and lax.ppermute only.
A program may use at most 128 MiB of HBM per device.

v0:
```python
import jax
import jax.numpy as jnp
from jax import lax
from jax.sharding import PartitionSpec as P

BLK = 128


def passed_along(block, axis, distance):
    devices = range(lax.axis_size(axis))
    route = [(i - distance, i) for i in devices if i - distance in devices]
    return lax.ppermute(block, axis, route)


def token_docs(doc_blocks, first_block, count, block):
    doc_ends = jnp.cumsum(doc_blocks, dtype=jnp.int32)
    blocks = first_block + jnp.arange(count, dtype=jnp.int32)
    owners = jnp.sum(
        (doc_ends[None, :] <= blocks[:, None]).astype(jnp.int32), axis=1, dtype=jnp.int32
    )
    owners = jnp.where(blocks < 0, -1, owners)
    return jnp.repeat(owners, block)


def attend(query_tiles, offsets, key_buffer, value_buffer, key_docs, key_span):
    tile_rows = query_tiles.shape[1]
    width = key_span + tile_rows
    score_scale = query_tiles.shape[-1] ** (-0.5)
    causal = jnp.arange(width)[None, :] <= key_span + jnp.arange(tile_rows)[:, None]

    def one_tile(packed):
        query_tile, offset = packed
        key_window = lax.dynamic_slice_in_dim(key_buffer, offset, width, 0)
        value_window = lax.dynamic_slice_in_dim(value_buffer, offset, width, 0)
        window_docs = lax.dynamic_slice_in_dim(key_docs, offset, width, 0)
        query_docs = lax.dynamic_slice_in_dim(key_docs, offset + key_span, tile_rows, 0)
        allowed = (window_docs[None, :] == query_docs[:, None]) & causal
        scores = (
            jnp.einsum("qhd,kd->hqk", query_tile, key_window, preferred_element_type=jnp.float32)
            * score_scale
        )
        scores = jnp.where(allowed[None], scores, -jnp.inf)
        row_max = jnp.max(scores, axis=2, keepdims=True)
        weights = jnp.exp(scores - row_max)
        totals = jnp.sum(weights, axis=2)
        combined = jnp.einsum(
            "hqk,kd->qhd",
            weights.astype(jnp.bfloat16),
            value_window,
            preferred_element_type=jnp.float32,
        )
        return (combined / jnp.transpose(totals)[:, :, None]).astype(jnp.bfloat16)

    return lax.map(one_tile, (query_tiles, offsets))


def on_device(queries, keys, values, doc_blocks):
    tok_rows, head_count, head_size = queries.shape
    kv_heads = keys.shape[1]
    dp_count = lax.axis_size("dp")
    ctx_count = lax.axis_size("ctx")
    ctx_index = lax.axis_index("ctx")
    region = tok_rows * dp_count
    tile_rows = region // ctx_count
    key_span = region // 2
    heads_here = head_count // dp_count
    sharing = dp_count // kv_heads
    key_copies = jnp.repeat(keys, sharing, axis=1)
    value_copies = jnp.repeat(values, sharing, axis=1)
    query_local, key_local, value_local = (
        lax.all_to_all(queries, "dp", split_axis=1, concat_axis=0, tiled=True),
        lax.all_to_all(key_copies, "dp", split_axis=1, concat_axis=0, tiled=True),
        lax.all_to_all(value_copies, "dp", split_axis=1, concat_axis=0, tiled=True),
    )
    key_local = key_local.reshape(region, head_size)
    value_local = value_local.reshape(region, head_size)
    query_tiles = query_local.reshape(ctx_count, tile_rows, heads_here, head_size)
    key_tail = key_local[region - key_span :]
    value_tail = value_local[region - key_span :]
    key_before, value_before = passed_along((key_tail, value_tail), "ctx", 1)
    key_buffer = jnp.concatenate([key_before, key_local], axis=0)
    value_buffer = jnp.concatenate([value_before, value_local], axis=0)
    key_docs = token_docs(
        doc_blocks, (ctx_index * region - key_span) // BLK, (key_span + region) // BLK, BLK
    )
    offsets = jnp.arange(ctx_count, dtype=jnp.int32) * tile_rows
    output_tiles = attend(query_tiles, offsets, key_buffer, value_buffer, key_docs, key_span)
    output_region = output_tiles.reshape(region, heads_here, head_size)
    return lax.all_to_all(output_region, "dp", split_axis=0, concat_axis=1, tiled=True)


def solution(mesh):
    placed = (
        P(("ctx", "dp"), None, None),
        P(("ctx", "dp"), None, None),
        P(("ctx", "dp"), None, None),
        P(),
    )
    return jax.shard_map(
        on_device,
        mesh=mesh,
        in_specs=placed,
        out_specs=P(("ctx", "dp"), None, None),
        check_vma=False,
    )
```

profile of v0, /device:TPU:0, one launch (start us, length us, event | category | flops | bytes accessed | tf_op | source)
XLA Modules:
  0.0 90.9 jit_solution(9387972081525457675)
XLA Ops:
  0.0 1.7 %copy.46 = bf16[128,8,128]{2,0,1:T(8,128)(2,1)} copy(bf16[128,8,128]{2,1,0:T(8,128)(2,1)} %param.8) | data formatting | bytes 524288 | tf_op args[2]
  1.7 5.2 %all-to-all-start = ((bf16[128,8,128]{2,0,1:T(8,128)(2,1)}), bf16[128,8,128]{2,0,1:T(8,128)(2,1)S(1)}, u32[]{:S(2)}, u32[]{:S(2)}) async-start(bf16[128,8,128]{2,0,1:T(8,128)(2,1)} %copy.46), calls=%async_computation | async-start | bytes 524288 | tf_op jit(solution)/shard_map/all_to_all | solution.py:73
  6.9 0.7 copy.49
  7.7 1.7 %copy.50 = bf16[128,8,128]{2,0,1:T(8,128)(2,1)} copy(bf16[128,8,128]{2,1,0:T(8,128)(2,1)} %param.7) | data formatting | bytes 524288 | tf_op args[1]
  9.4 4.4 %all-to-all-done = bf16[128,8,128]{2,0,1:T(8,128)(2,1)S(1)} async-done(((bf16[128,8,128]{2,0,1:T(8,128)(2,1)}), bf16[128,8,128]{2,0,1:T(8,128)(2,1)S(1)}, u32[]{:S(2)}, u32[]{:S(2)}) %all-to-all-start) | async-done | bytes 262176 | tf_op jit(solution)/shard_map/all_to_all | solution.py:73
  13.8 3.4 %all-to-all-start.1 = ((bf16[128,8,128]{2,0,1:T(8,128)(2,1)}), bf16[128,8,128]{2,0,1:T(8,128)(2,1)S(1)}, u32[]{:S(2)}, u32[]{:S(2)}) async-start(bf16[128,8,128]{2,0,1:T(8,128)(2,1)} %copy.50), calls=%async_computation.1 | async-start | bytes 524288 | tf_op jit(solution)/shard_map/all_to_all | solution.py:72
  17.4 2.6 %copy.51 = bf16[128,32,128]{2,0,1:T(8,128)(2,1)} copy(bf16[128,32,128]{2,1,0:T(8,128)(2,1)} %param.6) | data formatting | bytes 2097152 | tf_op args[0]
  20.0 4.1 %all-to-all-done.1 = bf16[128,8,128]{2,0,1:T(8,128)(2,1)S(1)} async-done(((bf16[128,8,128]{2,0,1:T(8,128)(2,1)}), bf16[128,8,128]{2,0,1:T(8,128)(2,1)S(1)}, u32[]{:S(2)}, u32[]{:S(2)}) %all-to-all-start.1) | async-done | bytes 262176 | tf_op jit(solution)/shard_map/all_to_all | solution.py:72
  24.1 3.6 %all-to-all-start.2 = ((bf16[128,32,128]{2,0,1:T(8,128)(2,1)}), bf16[128,32,128]{2,0,1:T(8,128)(2,1)S(1)}, u32[]{:S(2)}, u32[]{:S(2)}) async-start(bf16[128,32,128]{2,0,1:T(8,128)(2,1)} %copy.51), calls=%async_computation.2 | async-start | bytes 2097152 | tf_op jit(solution)/shard_map/all_to_all | solution.py:71
  27.9 3.5 %collective-permute-start = (bf16[512,128]{0,1:T(8,128)(2,1)S(1)}, bf16[512,128]{0,1:T(8,128)(2,1)S(1)}, u32[]{:S(2)}, u32[]{:S(2)}) collective-permute-start(bf16[512,128]{0,1:T(8,128)(2,1)S(1)} %copy.47), channel_id=1, source_target_pairs={{0,1},{1,2},{2,3},{4,5},{5,6},{6,7},{8,9},{9,10},{10,11},{12,13},{... | collective-permute-start | bytes 393224 | tf_op jit(solution)/shard_map/ppermute | solution.py:12
  31.6 3.5 %collective-permute-start.1 = (bf16[512,128]{1,0:T(8,128)(2,1)S(1)}, bf16[512,128]{1,0:T(8,128)(2,1)S(1)}, u32[]{:S(2)}, u32[]{:S(2)}) collective-permute-start(bf16[512,128]{1,0:T(8,128)(2,1)S(1)} %bitcast.98), channel_id=1, source_target_pairs={{0,1},{1,2},{2,3},{4,5},{5,6},{6,7},{8,9},{9,10},{10,11},{12,13},{... | collective-permute-start | bytes 393224 | tf_op jit(solution)/shard_map/ppermute | solution.py:12
  35.1 0.8 pad_maximum_fusion
  35.8 2.3 %collective-permute-done.1 = bf16[512,128]{1,0:T(8,128)(2,1)S(1)} collective-permute-done((bf16[512,128]{1,0:T(8,128)(2,1)S(1)}, bf16[512,128]{1,0:T(8,128)(2,1)S(1)}, u32[]{:S(2)}, u32[]{:S(2)}) %collective-permute-start.1) | collective-permute-done | bytes 131104 | tf_op jit(solution)/shard_map/ppermute | solution.py:12
  38.1 4.9 %all-to-all-done.2 = bf16[128,32,128]{2,0,1:T(8,128)(2,1)S(1)} async-done(((bf16[128,32,128]{2,0,1:T(8,128)(2,1)}), bf16[128,32,128]{2,0,1:T(8,128)(2,1)S(1)}, u32[]{:S(2)}, u32[]{:S(2)}) %all-to-all-start.2) | async-done | bytes 1048608 | tf_op jit(solution)/shard_map/all_to_all | solution.py:71
  43.1 27.3 %while.13 = (s32[]{:T(128)}, bf16[4,256,4,128]{3,1,0,2:T(8,128)(2,1)S(1)}, s32[4]{0:T(128)S(1)}, bf16[1536,128]{0,1:T(8,128)(2,1)}, s32[1536]{0:T(1024)S(1)}, /*...) while((s32[]{:T(128)}, ...), condition=%wide.region_5.6_spmd.clone, body=%wide.region_2.5_spmd.clone.sunk | while | flops 412153856 | bytes 13796621 | solution.py:54
  47.3 0.7 fusion.41
  48.7 1.0 %fusion.43 = bf16[1,256,4,128]{1,3,2,0:T(8,128)(2,1)S(1)} fusion(f32[768,256,4]{1,0,2:T(8,128)S(1)} %get-tuple-element.227, f32[4,256]{1,0:T(4,128)S(1)} %get-tuple-element.228, pred[256,768]{0,1:T(8,128)(4,1)S(1)} %fusion.40, f32[256,4]{0,1:T(4,128)S(1)} %bitcast.99, bf16[1536,128]{0,1:T(8,128)(2,1)S(1)} %copy-done, s32[]{:T(128)S(6)} %select_n.61), kind=kOutput, calls=%fused_computation.11.clone.1 | convolution fusion | flops 204734464 | bytes 3809284 | tf_op jit(solution)/shard_map/while/body/eval_jaxpr/hqk,kd->qhd/dot_general | solution.py:46
  55.5 1.0 %fusion.43 = bf16[1,256,4,128]{1,3,2,0:T(8,128)(2,1)S(1)} fusion(f32[768,256,4]{1,0,2:T(8,128)S(1)} %get-tuple-element.227, f32[4,256]{1,0:T(4,128)S(1)} %get-tuple-element.228, pred[256,768]{0,1:T(8,128)(4,1)S(1)} %fusion.40, f32[256,4]{0,1:T(4,128)S(1)} %bitcast.99, bf16[1536,128]{0,1:T(8,128)(2,1)S(1)} %copy-done, s32[]{:T(128)S(6)} %select_n.61), kind=kOutput, calls=%fused_computation.11.clone.1 | convolution fusion | flops 204734464 | bytes 3809284 | tf_op jit(solution)/shard_map/while/body/eval_jaxpr/hqk,kd->qhd/dot_general | solution.py:46
  62.4 1.0 %fusion.43 = bf16[1,256,4,128]{1,3,2,0:T(8,128)(2,1)S(1)} fusion(f32[768,256,4]{1,0,2:T(8,128)S(1)} %get-tuple-element.227, f32[4,256]{1,0:T(4,128)S(1)} %get-tuple-element.228, pred[256,768]{0,1:T(8,128)(4,1)S(1)} %fusion.40, f32[256,4]{0,1:T(4,128)S(1)} %bitcast.99, bf16[1536,128]{0,1:T(8,128)(2,1)S(1)} %copy-done, s32[]{:T(128)S(6)} %select_n.61), kind=kOutput, calls=%fused_computation.11.clone.1 | convolution fusion | flops 204734464 | bytes 3809284 | tf_op jit(solution)/shard_map/while/body/eval_jaxpr/hqk,kd->qhd/dot_general | solution.py:46
  67.8 0.7 fusion.41
  69.2 1.0 %fusion.43 = bf16[1,256,4,128]{1,3,2,0:T(8,128)(2,1)S(1)} fusion(f32[768,256,4]{1,0,2:T(8,128)S(1)} %get-tuple-element.227, f32[4,256]{1,0:T(4,128)S(1)} %get-tuple-element.228, pred[256,768]{0,1:T(8,128)(4,1)S(1)} %fusion.40, f32[256,4]{0,1:T(4,128)S(1)} %bitcast.99, bf16[1536,128]{0,1:T(8,128)(2,1)S(1)} %copy-done, s32[]{:T(128)S(6)} %select_n.61), kind=kOutput, calls=%fused_computation.11.clone.1 | convolution fusion | flops 204734464 | bytes 3809284 | tf_op jit(solution)/shard_map/while/body/eval_jaxpr/hqk,kd->qhd/dot_general | solution.py:46
  70.4 0.8 copy.55
  71.2 17.8 %all_to_all.63 = bf16[1024,4,128]{2,1,0:T(4,128)(2,1)S(1)} all-to-all(bf16[1024,4,128]{2,1,0:T(4,128)(2,1)S(1)} %copy.55), channel_id=1, replica_groups=mesh['dp'=8,'ctx'=4] {'dp'}, dimensions={0} | all-to-all | bytes 2097152 | tf_op jit(solution)/shard_map/all_to_all | solution.py:89
  89.3 1.7 %copy.58 = bf16[128,32,128]{2,1,0:T(8,128)(2,1)} copy(bf16[128,32,128]{2,0,1:T(8,128)(2,1)S(1)} %bitcast.91) | data formatting | bytes 2097152 | tf_op jit(solution)/shard_map/all_to_all | solution.py:89
  (56 shorter events, 9.8 us)
Async XLA Ops:
  1.7 12.1 %all-to-all-start = ((bf16[128,8,128]{2,0,1:T(8,128)(2,1)}), bf16[128,8,128]{2,0,1:T(8,128)(2,1)S(1)}, u32[]{:S(2)}, u32[]{:S(2)}) async-start(bf16[128,8,128]{2,0,1:T(8,128)(2,1)} %copy.46), calls=%async_computation | async-start | bytes 524288 | tf_op jit(solution)/shard_map/all_to_all | solution.py:73
  13.8 10.3 %all-to-all-start.1 = ((bf16[128,8,128]{2,0,1:T(8,128)(2,1)}), bf16[128,8,128]{2,0,1:T(8,128)(2,1)S(1)}, u32[]{:S(2)}, u32[]{:S(2)}) async-start(bf16[128,8,128]{2,0,1:T(8,128)(2,1)} %copy.50), calls=%async_computation.1 | async-start | bytes 524288 | tf_op jit(solution)/shard_map/all_to_all | solution.py:72
  24.1 18.9 %all-to-all-start.2 = ((bf16[128,32,128]{2,0,1:T(8,128)(2,1)}), bf16[128,32,128]{2,0,1:T(8,128)(2,1)S(1)}, u32[]{:S(2)}, u32[]{:S(2)}) async-start(bf16[128,32,128]{2,0,1:T(8,128)(2,1)} %copy.51), calls=%async_computation.2 | async-start | bytes 2097152 | tf_op jit(solution)/shard_map/all_to_all | solution.py:71
  27.9 7.2 %collective-permute-start = (bf16[512,128]{0,1:T(8,128)(2,1)S(1)}, bf16[512,128]{0,1:T(8,128)(2,1)S(1)}, u32[]{:S(2)}, u32[]{:S(2)}) collective-permute-start(bf16[512,128]{0,1:T(8,128)(2,1)S(1)} %copy.47), channel_id=1, source_target_pairs={{0,1},{1,2},{2,3},{4,5},{5,6},{6,7},{8,9},{9,10},{10,11},{12,13},{... | collective-permute-start | bytes 393224 | tf_op jit(solution)/shard_map/ppermute | solution.py:12
  31.6 6.5 %collective-permute-start.1 = (bf16[512,128]{1,0:T(8,128)(2,1)S(1)}, bf16[512,128]{1,0:T(8,128)(2,1)S(1)}, u32[]{:S(2)}, u32[]{:S(2)}) collective-permute-start(bf16[512,128]{1,0:T(8,128)(2,1)S(1)} %bitcast.98), channel_id=1, source_target_pairs={{0,1},{1,2},{2,3},{4,5},{5,6},{6,7},{8,9},{9,10},{10,11},{12,13},{... | collective-permute-start | bytes 393224 | tf_op jit(solution)/shard_map/ppermute | solution.py:12
  47.3 1.4 %copy-start = (bf16[1536,128]{0,1:T(8,128)(2,1)S(1)}, bf16[1536,128]{0,1:T(8,128)(2,1)}, u32[]{:S(2)}) copy-start(bf16[1536,128]{0,1:T(8,128)(2,1)} %get-tuple-element.258) | copy-start | bytes 1179652 | tf_op jit(solution)/shard_map/while
  54.1 1.4 %copy-start = (bf16[1536,128]{0,1:T(8,128)(2,1)S(1)}, bf16[1536,128]{0,1:T(8,128)(2,1)}, u32[]{:S(2)}) copy-start(bf16[1536,128]{0,1:T(8,128)(2,1)} %get-tuple-element.258) | copy-start | bytes 1179652 | tf_op jit(solution)/shard_map/while
  61.0 1.4 %copy-start = (bf16[1536,128]{0,1:T(8,128)(2,1)S(1)}, bf16[1536,128]{0,1:T(8,128)(2,1)}, u32[]{:S(2)}) copy-start(bf16[1536,128]{0,1:T(8,128)(2,1)} %get-tuple-element.258) | copy-start | bytes 1179652 | tf_op jit(solution)/shard_map/while
  67.8 1.4 %copy-start = (bf16[1536,128]{0,1:T(8,128)(2,1)S(1)}, bf16[1536,128]{0,1:T(8,128)(2,1)}, u32[]{:S(2)}) copy-start(bf16[1536,128]{0,1:T(8,128)(2,1)} %get-tuple-element.258) | copy-start | bytes 1179652 | tf_op jit(solution)/shard_map/while
where the time goes:
time: 91.7 us; the launch traced here: 90.9 us
  starting transfers between devices  19.1 us (21%)
  blocking collectives  17.8 us (19%)
  waiting for transfers between devices  15.6 us (17%)
  local copies, waits for them, and re-layouts  13.7 us (15%)
  loops' own time  13.2 us (14%)
  matrix products  6.73 us (7%)
  other arithmetic  4.65 us (5%)
    all_to_all x1, blocking collectives, on_device(): lax.all_to_all(output_region, 'dp', split_axis=0, concat_axis=1, tiled=True)  17.8 us
    another operation x1, loops' own time, attend(): return lax.map(one_tile, (query_tiles, offsets))  13.2 us
    ppermute x2, starting transfers between devices, passed_along(): return lax.ppermute(block, axis, route)  6.97 us
    unnamed x3, local copies, waits for them, and re-layouts  5.97 us
    all_to_all x1, starting transfers between devices, on_device(): lax.all_to_all(value_copies, 'dp', split_axis=1, concat_axis=0, tiled=True)  5.17 us
    all_to_all x1, waiting for transfers between devices, on_device(): lax.all_to_all(queries, 'dp', split_axis=1, concat_axis=0, tiled=True)  4.87 us
    all_to_all x1, waiting for transfers between devices, on_device(): lax.all_to_all(value_copies, 'dp', split_axis=1, concat_axis=0, tiled=True)  4.37 us
    all_to_all x1, waiting for transfers between devices, on_device(): lax.all_to_all(key_copies, 'dp', split_axis=1, concat_axis=0, tiled=True)  4.07 us
  transfers between devices with their start and end apart: 5, of which 4 were waited for; matrix products, arithmetic and copies ran while one was open for 7% of the time, Pallas kernels for 0%

commit v1 on v0

v1 whole, which is shorter than its diff:
```python
import functools

import jax
import jax.numpy as jnp
from jax import lax
from jax.experimental import pallas as pl
from jax.experimental.pallas import tpu as pltpu
from jax.sharding import PartitionSpec as P

LOG2E = 1.4426950408889634
MIB = 1 << 20
VMEM = pl.BlockSpec(memory_space=pltpu.VMEM)
SMEM = pl.BlockSpec(memory_space=pltpu.SMEM)
ANY = pl.BlockSpec(memory_space=pl.ANY)
HBM = pl.BlockSpec(memory_space=pltpu.HBM)
LANES = 128
GROUP = 4
EIGHT = 2 * GROUP
TILE = 64


def pack_kernel(k_ref, v_ref, out_ref, longer_ref, keys_ref, values_ref, near, wide, sems):
    _, rows, heads, size = near.shape
    copies = [pltpu.make_async_copy(ref, near.at[n], sems.at[n]) for n, ref in enumerate((k_ref, v_ref))]
    for copy in copies:
        copy.start()
    for n, copy in enumerate(copies):
        copy.wait()
        wide[n] = near[n].astype(jnp.float32).reshape(rows * heads, size)
        for g in range(heads):
            part = wide[n, pl.ds(g, rows, stride=heads), :].astype(jnp.bfloat16)
            part = part.T if n == 0 else part
            lanes = slice(g * size, (g + 1) * size)
            for ref in (out_ref, longer_ref):
                ref[n * rows : (n + 1) * rows, lanes] = part
            (keys_ref, values_ref)[n][:, lanes] = part


def pack(keys, values):
    rows, heads, size = keys.shape
    assert rows == size
    keys, values = (pltpu.with_memory_space_constraint(x, pltpu.HBM) for x in (keys, values))
    heights = 2 * rows, 2 * rows + 8, rows, rows
    return pl.pallas_call(
        pack_kernel,
        out_shape=tuple(jax.ShapeDtypeStruct((height, heads * size), jnp.bfloat16) for height in heights),
        in_specs=[HBM, HBM],
        out_specs=(VMEM,) * len(heights),
        scratch_shapes=[
            pltpu.VMEM((2, rows, heads, size), jnp.bfloat16),
            pltpu.VMEM((2, rows * heads, size), jnp.float32),
            pltpu.SemaphoreType.DMA((2,)),
        ],
        compiler_params=pltpu.CompilerParams(vmem_limit_bytes=8 * MIB),
        name="pack_kv",
    )(keys, values)


def blocks_before(doc_ref, block):
    def step(j, carry):
        end, start = carry
        end = end + doc_ref[j]
        return end, jnp.where(end <= block, end, start)

    _, start = lax.fori_loop(0, doc_ref.shape[0], step, (jnp.int32(0), jnp.int32(0)))
    return block - start


def low_rows(rows, lanes):
    return lax.broadcasted_iota(jnp.int32, (rows, lanes), 0) % EIGHT < GROUP


def keys_of(blocks, j, rows):
    at = 2 * j * rows
    pairs = [jnp.concatenate([ref[:rows, at : at + rows], ref[:rows, at + rows : at + 2 * rows]], axis=0) for ref, _ in blocks]
    return jnp.concatenate(pairs, axis=1)


def values_of(blocks, j, rows):
    lanes = slice(2 * j * rows, 2 * (j + 1) * rows)
    tops = [rows if ref.shape[0] > rows else 0 for _, ref in blocks]
    return jnp.concatenate([ref[top : top + rows, lanes] for top, (_, ref) in zip(tops, blocks)], axis=0)


def dot(a, b):
    return jnp.dot(a, b, preferred_element_type=jnp.float32)


def prepare_kernel(doc_ref, q_ref, lhs_ref, before_ref, lengths, near, sems):
    rows, heads, size = near.shape
    tall = TILE * EIGHT
    low = low_rows(tall, size)
    spans = [pl.ds(t * TILE, TILE) for t in range(rows // TILE)]
    copies = [pltpu.make_async_copy(doc_ref, lengths, sems.at[len(spans)])]
    copies += [pltpu.make_async_copy(q_ref.at[span], near.at[span], sems.at[t]) for t, span in enumerate(spans)]
    for copy in copies:
        copy.start()
    copies[0].wait()
    block = lax.axis_index("ctx") * lax.axis_size("dp") + lax.axis_index("dp")
    before_ref[...] = jnp.full(before_ref.shape, blocks_before(lengths, block), jnp.int32)
    for t, span in enumerate(spans):
        copies[1 + t].wait()
        for j in range(heads // EIGHT):
            if j % 2 == 0:
                q16 = near[span, j * EIGHT : (j + 2) * EIGHT, :].astype(jnp.float32)
            q8 = q16[:, j % 2 * EIGHT : (j % 2 + 1) * EIGHT, :].reshape(tall, size)
            lhs = jnp.concatenate([jnp.where(low, q8, 0.0), jnp.where(low, 0.0, q8)], axis=1)
            lhs_ref[j, t * tall : (t + 1) * tall, :] = lhs.astype(jnp.bfloat16)


def prepare(doc_blocks, queries):
    rows, heads, size = queries.shape
    doc_blocks, queries = (pltpu.with_memory_space_constraint(x, pltpu.HBM) for x in (doc_blocks, queries))
    return pl.pallas_call(
        prepare_kernel,
        out_shape=(
            jax.ShapeDtypeStruct((heads // EIGHT, rows * EIGHT, 2 * size), jnp.bfloat16),
            jax.ShapeDtypeStruct((EIGHT, LANES), jnp.int32),
        ),
        in_specs=[HBM, HBM],
        out_specs=(VMEM, VMEM),
        scratch_shapes=[
            pltpu.SMEM(doc_blocks.shape, jnp.int32),
            pltpu.VMEM(queries.shape, jnp.bfloat16),
            pltpu.SemaphoreType.DMA((rows // TILE + 1,)),
        ],
        compiler_params=pltpu.CompilerParams(vmem_limit_bytes=12 * MIB),
        cost_estimate=pl.CostEstimate(flops=1024, bytes_accessed=1024, transcendentals=0),
        name="prepare",
    )(doc_blocks, queries)


def attend_kernel(cases, scale, merges, keeps, gives, blocks_of, *refs):
    refs = list(refs)
    lhs_ref, before_ref = refs[:2]
    del refs[:2]
    if merges:
        state_ref = refs[:3]
        del refs[:3]
    count = max(at for block in blocks_of for at in block) + 1
    given = [(refs[a], refs[b]) for a, b in blocks_of]
    del refs[:count]
    if gives == "given":
        del refs[0]
    if keeps:
        state_out = refs[:3]
        del refs[:3]
    if gives:
        out_ref, held, sems = refs
    js, size = lhs_ref.shape[0], lhs_ref.shape[2] // 2
    rows = lhs_ref.shape[1] // EIGHT
    place = lax.axis_index("dp")
    before = jnp.max(before_ref[...])

    def out_copy(t, tokens):
        return pltpu.make_async_copy(held.at[tokens], out_ref.at[tokens], sems.at[t])

    def add(blocks, last):
        tall = TILE * EIGHT
        low = low_rows(tall, size)
        if not merges:
            token = lax.broadcasted_iota(jnp.int32, (tall, rows), 0) // EIGHT
            spot = lax.broadcasted_iota(jnp.int32, (tall, rows), 1)
        for t in range(rows // TILE):
            tokens, here, outs = pl.ds(t * TILE, TILE), pl.ds(t * tall, tall), []
            for j in range(js):
                if merges:
                    old, total, mixed = (ref[j, here, :] for ref in state_ref)
                if blocks:
                    s = dot(lhs_ref[j, here, :], keys_of(blocks, j, rows))
                    s = [s[:, n * rows : (n + 1) * rows] for n in range(len(blocks))]
                    if not merges:
                        s[0] = jnp.where(spot <= token + t * TILE, s[0], -jnp.inf)
                    top = jnp.max(functools.reduce(jnp.maximum, s), axis=1, keepdims=True)
                    if merges:
                        top = jnp.maximum(old, top)
                        keep = jnp.exp2((old - top) * scale)
                    w = [jnp.exp2((part - top) * scale) for part in s]
                    found = dot(jnp.concatenate(w, axis=1).astype(jnp.bfloat16), values_of(blocks, j, rows))
                    found = jnp.where(low, found[:, :size], found[:, size:])
                    fresh = functools.reduce(jnp.add, w)
                    mixed = found + keep * mixed if merges else found
                    total = fresh + keep * total if merges else fresh
                if last:
                    total = jnp.sum(total, axis=1, keepdims=True)
                    guess = pl.reciprocal(total, approx=True)
                    guess = guess * (2.0 - total * guess)
                    outs.append((mixed * guess).reshape(TILE, EIGHT, size))
                    if j % 2:
                        held[tokens, (j - 1) * EIGHT : (j + 1) * EIGHT, :] = jnp.concatenate(
                            outs[-2:], axis=1
                        ).astype(jnp.bfloat16)
                else:
                    state_out[0][j, here, :] = jnp.broadcast_to(top, (tall, LANES))
                    state_out[1][j, here, :] = total
                    state_out[2][j, here, :] = mixed
            if last:
                out_copy(t, tokens).start()
        if last:
            for t in range(rows // TILE):
                out_copy(t, pl.ds(t * TILE, TILE)).wait()

    for wheres, chosen, last in cases:
        fits = False
        for parity, least, end in wheres:
            fit = before >= least
            if end is not None:
                fit = jnp.logical_and(fit, before < end)
            if parity is not None:
                fit = jnp.logical_and(fit, place % 2 == parity)
            fits = fit if fits is False else jnp.logical_or(fits, fit)
        pl.when(fits)(functools.partial(add, [given[at] for at in chosen], last))


def attend(name, shape, prepared, kvs, cases, state=(), keeps=False, gives="", given=None, in_place=False):
    rows, heads, size = shape
    js, tall = heads // EIGHT, rows * EIGHT
    arrays, blocks_of = [], []
    for block in kvs:
        block = block if isinstance(block, tuple) else (block,)
        blocks_of.append((len(arrays), len(arrays) + len(block) - 1))
        arrays += block
    inputs = [*prepared, *state, *arrays]
    specs = [VMEM] * len(inputs)
    outs = [jax.ShapeDtypeStruct((js, tall, LANES), jnp.float32)] * (3 if keeps else 0)
    out_specs = [VMEM] * len(outs)
    aliases = {2: 0, 3: 1, 4: 2} if in_place else {}
    if gives == "given":
        aliases[len(inputs)] = len(outs)
        inputs.append(given)
        specs.append(ANY)
    if gives:
        outs.append(jax.ShapeDtypeStruct(shape, jnp.bfloat16))
        out_specs.append(ANY)
    scale = LOG2E * size ** (-0.5)
    return pl.pallas_call(
        functools.partial(attend_kernel, cases, scale, bool(state), keeps, gives, blocks_of),
        out_shape=tuple(outs),
        in_specs=specs,
        out_specs=tuple(out_specs),
        input_output_aliases=aliases,
        scratch_shapes=[pltpu.VMEM(shape, jnp.bfloat16), pltpu.SemaphoreType.DMA((rows // TILE,))] if gives else [],
        compiler_params=pltpu.CompilerParams(vmem_limit_bytes=24 * MIB),
        cost_estimate=pl.CostEstimate(flops=1024, bytes_accessed=1024, transcendentals=0),
        name=name,
    )(*inputs)


def on_device(axes, dp, ctx, queries, keys, values, doc_blocks):
    own, longer, own_keys, own_values = pack(keys, values)
    count, farthest = dp * ctx, dp // 2 - 1
    def moved(array, target_of):
        def at(block):
            return block % dp * ctx + block // dp if axes[0] == "dp" else block

        route = [(i, target_of(i)) for i in range(count)]
        return lax.ppermute(array, axes, [(at(i), at(to)) for i, to in route if to is not None and to < count])

    if farthest == 3:
        crossed = moved(own, lambda i: i + 1 if i % 2 else i + 3)
        beside = tuple(moved(part, lambda i: None if i % 2 else i + 1) for part in (own_keys, own_values))
        queries, beside = lax.optimization_barrier((queries, beside))
        prepared = prepare(doc_blocks, queries)
        call = functools.partial(attend, shape=queries.shape, prepared=prepared)
        *state, out = call(
            "own_blocks",
            kvs=[own, beside],
            cases=[
                ([(None, 0, 1)], [0], True),
                ([(1, 1, 2)], [0, 1], True),
                ([(0, 1, None)], [0], False),
                ([(1, 2, None)], [0, 1], False),
            ],
            keeps=True,
            gives="fresh",
        )
        longer, out = lax.optimization_barrier((longer, out))
        behind = moved(longer, lambda i: i + 3 if i % 2 else None)
        crossed, out = lax.optimization_barrier((crossed, out))
        swapped = moved(crossed, lambda i: i ^ 1)
        (out,) = call("nearest", kvs=[own, crossed], cases=[([(0, 1, 2)], [0, 1], True)], gives="given", given=out)
        *state, out = call(
            "swapped_blocks",
            kvs=[crossed, swapped],
            cases=[
                ([(0, 2, 3), (1, 3, None)], [0, 1], True),
                ([(0, 3, None)], [0, 1], False),
                ([(1, 2, 3)], [1], True),
            ],
            state=state,
            keeps=True,
            gives="given",
            given=out,
        )
        (out,) = call(
            "farthest", kvs=[behind], cases=[([(0, 3, None)], [0], True)], state=state, gives="given", given=out
        )
        return out
    call = functools.partial(attend, shape=queries.shape, prepared=prepare(doc_blocks, queries))
    state = call("own_blocks", kvs=[own], cases=[([(None, 0, None)], [0], False)], keeps=True)
    shifted = [moved(own, lambda i, m=m: i + 2 * m) for m in range(1, (farthest - 1) // 2 + 1)]
    alone = moved(longer, lambda i: i + farthest if i % 2 else i + 1)
    shifted, state = lax.optimization_barrier((shifted, state))
    for m, block in enumerate(shifted, 1):
        other = moved(block, lambda i: i ^ 1)
        cases = [
            ([(0, 2 * m - 1, 2 * m)], [1], False),
            ([(0, 2 * m, None), (1, 2 * m + 1, None)], [0, 1], False),
            ([(1, 2 * m, 2 * m + 1)], [0], False),
        ]
        state = call("more_blocks", kvs=[block, other], cases=cases, state=state, keeps=True, in_place=True)
    cases = [
        ([(0, farthest, None), (1, 1, None)], [0], True),
        ([(0, 0, farthest), (1, 0, 1)], [], True),
    ]
    (out,) = call("farthest", kvs=[alone], cases=cases, state=state, gives="fresh")
    return out


def solution(mesh):
    dp, ctx = mesh.shape["dp"], mesh.shape["ctx"]
    placed = P(("ctx", "dp"), None, None)
    return jax.shard_map(
        functools.partial(on_device, tuple(mesh.axis_names), dp, ctx),
        mesh=mesh,
        in_specs=(placed, placed, placed, P()),
        out_specs=placed,
        check_vma=False,
    )
```

time: 91.7 us -> 27.4 us (0.30)
  the two profiles are of different devices: /device:TPU:0 before, /device:TPU:4 now
where the time goes in v1:
time: 27.4 us; the launch traced here: 27.7 us
  Pallas kernels  10.6 us (39%)
  waiting for transfers between devices  8.73 us (32%)
  starting transfers between devices  8.05 us (29%)
    ppermute x5, waiting for transfers between devices, moved(): lax.ppermute(array, axes, [(at(i), at(to)) for i, to in route if to is no...  8.73 us
    ppermute x5, starting transfers between devices, moved(): lax.ppermute(array, axes, [(at(i), at(to)) for i, to in route if to is no...  8.05 us
    pallas_call x4, Pallas kernels, attend(): pl.pallas_call(functools.partial(attend_kernel, cases, scale, bool(state)...  7.8 us
    pallas_call x1, Pallas kernels, prepare(): pl.pallas_call(prepare_kernel, out_shape=(jax.ShapeDtypeStruct((heads //...  1.42 us
    pallas_call x1, Pallas kernels, pack(): pl.pallas_call(pack_kernel, out_shape=tuple((jax.ShapeDtypeStruct((height...  1.4 us
  transfers between devices with their start and end apart: 5, of which 4 were waited for; matrix products, arithmetic and copies ran while one was open for 0% of the time, Pallas kernels for 21%

profile of v1, /device:TPU:4, one launch (start us, length us, event | category | flops | bytes accessed | tf_op | source)
XLA Modules:
  0.0 27.7 jit_solution(18200473874292786595)
XLA Ops:
  0.0 1.4 %pack_kv.1 = (bf16[256,1024]{1,0:T(8,128)(2,1)S(1)}, bf16[264,1024]{1,0:T(8,128)(2,1)S(1)}, bf16[128,1024]{1,0:T(8,128)(2,1)S(1)}, bf16[128,1024]{1,0:T(8,128)(2,1)S(1)}) custom-call(bf16[128,8,128]{2,1,0:T(8,128)(2,1)} %k_ref.1, bf16[128,8,128]{2,1,0:T(8,128)(2,1)} %v_ref.1), custom_call_target="tpu_custom_call" | custom-call | tf_op jit(solution)/shard_map/pack_kv/pallas_call | solution.py:44
  1.4 2.8 %collective-permute-start.2 = (bf16[256,1024]{1,0:T(8,128)(2,1)S(1)}, bf16[256,1024]{1,0:T(8,128)(2,1)S(1)}, u32[]{:S(2)}, u32[]{:S(2)}) collective-permute-start(bf16[256,1024]{1,0:T(8,128)(2,1)S(1)} %get-tuple-element.31.refs_2_), channel_id=1, source_target_pairs={{0,12},{4,8},{8,20},{12,16},{16,28},{20,24},{24,5},{28,1},{1,13},{... | collective-permute-start | bytes 1572872 | tf_op jit(solution)/shard_map/ppermute | solution.py:257
  4.3 2.6 %collective-permute-start = (bf16[128,1024]{1,0:T(8,128)(2,1)S(1)}, bf16[128,1024]{1,0:T(8,128)(2,1)S(1)}, u32[]{:S(2)}, u32[]{:S(2)}) collective-permute-start(bf16[128,1024]{1,0:T(8,128)(2,1)S(1)} %get-tuple-element.26), channel_id=1, source_target_pairs={{0,4},{8,12},{16,20},{24,28},{1,5},{9,13},{17,21},{25,29},{2,6},{1... | collective-permute-start | bytes 786440 | tf_op jit(solution)/shard_map/ppermute | solution.py:257
  6.9 1.3 %collective-permute-start.1 = (bf16[128,1024]{1,0:T(8,128)(2,1)S(1)}, bf16[128,1024]{1,0:T(8,128)(2,1)S(1)}, u32[]{:S(2)}, u32[]{:S(2)}) collective-permute-start(bf16[128,1024]{1,0:T(8,128)(2,1)S(1)} %get-tuple-element.27), channel_id=1, source_target_pairs={{0,4},{8,12},{16,20},{24,28},{1,5},{9,13},{17,21},{25,29},{2,6},{1... | collective-permute-start | bytes 786440 | tf_op jit(solution)/shard_map/ppermute | solution.py:257
  8.2 0.0 collective-permute-done.refs_3_
  8.2 1.1 %collective-permute-done.1.refs_4_ = bf16[128,1024]{1,0:T(8,128)(2,1)S(1)} collective-permute-done((bf16[128,1024]{1,0:T(8,128)(2,1)S(1)}, bf16[128,1024]{1,0:T(8,128)(2,1)S(1)}, u32[]{:S(2)}, u32[]{:S(2)}) %collective-permute-start.1) | collective-permute-done | bytes 262176 | tf_op jit(solution)/shard_map/ppermute | solution.py:257
  9.3 1.4 %prepare.1 = (bf16[4,1024,256]{2,1,0:T(8,128)(2,1)S(1)}, s32[8,128]{1,0:T(8,128)S(1)}) custom-call(s32[16]{0:T(128)} %doc_ref.1, bf16[128,32,128]{2,1,0:T(8,128)(2,1)} %q_ref), custom_call_target="tpu_custom_call" | custom-call | flops 1024 | bytes 1024 | tf_op jit(solution)/shard_map/prepare/pallas_call | solution.py:114
  10.7 1.9 %own_blocks.1 = (f32[4,1024,128]{2,1,0:T(8,128)S(1)}, f32[4,1024,128]{2,1,0:T(8,128)S(1)}, f32[4,1024,128]{2,1,0:T(8,128)S(1)}, bf16[128,32,128]{2,1,0:T(8,128)(2,1)}) custom-call(bf16[4,1024,256]{2,1,0:T(8,128)(2,1)S(1)} %get-tuple-element.29.refs_0_, s32[8,128]{1,0:T(8,128)S(1)} %get-tuple-element.30.refs_1_, ...), custom_call_target="tpu_custom_call" | custom-call | flops 1024 | bytes 1024 | tf_op jit(solution)/shard_map/own_blocks/pallas_call | solution.py:236
  12.6 1.3 %collective-permute-start.4 = (bf16[264,1024]{1,0:T(8,128)(2,1)S(1)}, bf16[264,1024]{1,0:T(8,128)(2,1)S(1)}, u32[]{:S(2)}, u32[]{:S(2)}) collective-permute-start(bf16[264,1024]{1,0:T(8,128)(2,1)S(1)} %get-tuple-element.45), channel_id=1, source_target_pairs={{4,16},{12,24},{20,1},{28,9},{5,17},{13,25},{21,2},{29,10},{6,18},... | collective-permute-start | bytes 1622024 | tf_op jit(solution)/shard_map/ppermute | solution.py:257
  13.9 4.6 %collective-permute-done.2.refs_3_.refs_5_ = bf16[256,1024]{1,0:T(8,128)(2,1)S(1)} collective-permute-done((bf16[256,1024]{1,0:T(8,128)(2,1)S(1)}, bf16[256,1024]{1,0:T(8,128)(2,1)S(1)}, u32[]{:S(2)}, u32[]{:S(2)}) %collective-permute-start.2) | collective-permute-done | bytes 524320 | tf_op jit(solution)/shard_map/ppermute | solution.py:257
  18.5 0.0 collective-permute-start.3
  18.5 0.2 nearest.1.refs_7_
  18.8 1.7 %collective-permute-done.3.refs_6_ = bf16[256,1024]{1,0:T(8,128)(2,1)S(1)} collective-permute-done((bf16[256,1024]{1,0:T(8,128)(2,1)S(1)}, bf16[256,1024]{1,0:T(8,128)(2,1)S(1)}, u32[]{:S(2)}, u32[]{:S(2)}) %collective-permute-start.3) | collective-permute-done | bytes 524320 | tf_op jit(solution)/shard_map/ppermute | solution.py:257
  20.4 2.4 %swapped_blocks.1 = (f32[4,1024,128]{2,1,0:T(8,128)S(1)}, f32[4,1024,128]{2,1,0:T(8,128)S(1)}, f32[4,1024,128]{2,1,0:T(8,128)S(1)}, bf16[128,32,128]{2,1,0:T(8,128)(2,1)}) custom-call(bf16[4,1024,256]{2,1,0:T(8,128)(2,1)S(1)} %get-tuple-element.29.refs_0_, s32[8,128]{1,0:T(8,128)S(1)} %get-tuple-element.30.refs_1_, ...), custom_call_target="tpu_custom_call", output_to_operand_aliasing={{3}: (7, {})} | custom-call | flops 1024 | bytes 1024 | tf_op jit(solution)/shard_map/swapped_blocks/pallas_call | solution.py:236
  22.8 1.4 %collective-permute-done.4.refs_5_ = bf16[264,1024]{1,0:T(8,128)(2,1)S(1)} collective-permute-done((bf16[264,1024]{1,0:T(8,128)(2,1)S(1)}, bf16[264,1024]{1,0:T(8,128)(2,1)S(1)}, u32[]{:S(2)}, u32[]{:S(2)}) %collective-permute-start.4) | collective-permute-done | bytes 540704 | tf_op jit(solution)/shard_map/ppermute | solution.py:257
  24.2 3.3 %farthest.1 = bf16[128,32,128]{2,1,0:T(8,128)(2,1)} custom-call(bf16[4,1024,256]{2,1,0:T(8,128)(2,1)S(1)} %get-tuple-element.29.refs_0_, s32[8,128]{1,0:T(8,128)S(1)} %get-tuple-element.30.refs_1_, f32[4,1024,128]{2,1,0:T(8,128)S(1)} %get-tuple-element.42.refs_2_, f32[4,1024,128]{2,1,0:T(8,128)S(1)} %get-tuple-element.43.refs_3_, ...), custom_call_target="tpu_custom_call", output_to_operand_aliasing={{}: (6, {})} | custom-call | flops 1024 | bytes 1024 | tf_op jit(solution)/shard_map/farthest/pallas_call | solution.py:236
Async XLA Ops:
  1.4 17.1 %collective-permute-start.2 = (bf16[256,1024]{1,0:T(8,128)(2,1)S(1)}, bf16[256,1024]{1,0:T(8,128)(2,1)S(1)}, u32[]{:S(2)}, u32[]{:S(2)}) collective-permute-start(bf16[256,1024]{1,0:T(8,128)(2,1)S(1)} %get-tuple-element.31.refs_2_), channel_id=1, source_target_pairs={{0,12},{4,8},{8,20},{12,16},{16,28},{20,24},{24,5},{28,1},{1,13},{... | collective-permute-start | bytes 1572872 | tf_op jit(solution)/shard_map/ppermute | solution.py:257
  4.3 3.9 %collective-permute-start = (bf16[128,1024]{1,0:T(8,128)(2,1)S(1)}, bf16[128,1024]{1,0:T(8,128)(2,1)S(1)}, u32[]{:S(2)}, u32[]{:S(2)}) collective-permute-start(bf16[128,1024]{1,0:T(8,128)(2,1)S(1)} %get-tuple-element.26), channel_id=1, source_target_pairs={{0,4},{8,12},{16,20},{24,28},{1,5},{9,13},{17,21},{25,29},{2,6},{1... | collective-permute-start | bytes 786440 | tf_op jit(solution)/shard_map/ppermute | solution.py:257
  6.9 2.4 %collective-permute-start.1 = (bf16[128,1024]{1,0:T(8,128)(2,1)S(1)}, bf16[128,1024]{1,0:T(8,128)(2,1)S(1)}, u32[]{:S(2)}, u32[]{:S(2)}) collective-permute-start(bf16[128,1024]{1,0:T(8,128)(2,1)S(1)} %get-tuple-element.27), channel_id=1, source_target_pairs={{0,4},{8,12},{16,20},{24,28},{1,5},{9,13},{17,21},{25,29},{2,6},{1... | collective-permute-start | bytes 786440 | tf_op jit(solution)/shard_map/ppermute | solution.py:257
  12.6 11.6 %collective-permute-start.4 = (bf16[264,1024]{1,0:T(8,128)(2,1)S(1)}, bf16[264,1024]{1,0:T(8,128)(2,1)S(1)}, u32[]{:S(2)}, u32[]{:S(2)}) collective-permute-start(bf16[264,1024]{1,0:T(8,128)(2,1)S(1)} %get-tuple-element.45), channel_id=1, source_target_pairs={{4,16},{12,24},{20,1},{28,9},{5,17},{13,25},{21,2},{29,10},{6,18},... | collective-permute-start | bytes 1622024 | tf_op jit(solution)/shard_map/ppermute | solution.py:257
  18.5 1.9 %collective-permute-start.3 = (bf16[256,1024]{1,0:T(8,128)(2,1)S(1)}, bf16[256,1024]{1,0:T(8,128)(2,1)S(1)}, u32[]{:S(2)}, u32[]{:S(2)}) collective-permute-start(bf16[256,1024]{1,0:T(8,128)(2,1)S(1)} %collective-permute-done.2.refs_3_.refs_5_), channel_id=1, source_target_pairs={{0,4},{4,0},{8,12},{12,8},{16,20},{20,16},{24,28},{28,24},{1,5},{5... | collective-permute-start | bytes 1572872 | tf_op jit(solution)/shard_map/ppermute | solution.py:257
